TPU v7x, 32 devices: a whole 2x2x4 slice. The times are simulated.
32 devices in a mesh: groups: 2 (over x), row: 16 (over z, y, core).
Axes of the slice: x: 2, y: 2, z: 4, core: 2. Of those that a mesh axis runs over, the one named last changes fastest.
Arguments:
- partner_aux_tiles: bfloat16 [256, 64, 1024], P(('groups', 'row')), parts along dimension 0, may hold values from -0.1875 to 0.1875
- row_aux_tiles: bfloat16 [256, 64, 1024], P(('groups', 'row')), parts along dimension 0, may hold values from -6 to 6
- tile_partner: int32 [256], P(('groups', 'row')), parts along dimension 0, may hold values from 0 to 15, as said below
- tile_count: int32 [32], P(('groups', 'row')), parts along dimension 0, may hold values from 1 to 8
- density_blocks: bfloat16 [256, 64, 64], P(('groups', 'row')), parts along dimension 0, may hold values from -0.25 to 0.25
- density_cols: int32 [256], P(('groups', 'row')), parts along dimension 0, may hold values from 0 to 15, as said below
- density_count: int32 [32], P(('groups', 'row')), parts along dimension 0, may hold values from 1 to 8
Outputs:
- exchange_window: float32 [2048, 704], P(('groups', 'row')), parts along dimension 0
There are 2 independent parts, one for each index of `groups`. A program takes and returns all parts, laid end to end along the dimension named above; each array names one. Nothing has to cross between parts.
Inputs may be any that keep to these rules, and one draw needn't show every extreme that they name: `tile_partner`: the 8 slots of one row block name distinct atom blocks within 5 blocks of it along the periodic order of 16 blocks. `density_cols`: the 8 slots of one row block name distinct atom blocks within 5 blocks of it along the periodic order of 16 blocks.
All inputs are finite; a program needn't handle non-finite values.
Results may differ from a plain program's by a relative error of at most 0.0029.
Values may be sent and summed in bfloat16 or wider, within the bound.
A program may use at most 64 MiB of HBM per device.

v0:
```python
import jax
import jax.numpy as jnp
from jax import lax
from jax.sharding import PartitionSpec as P

REACH = 5


def passed_along(block, axis, distance):
    devices = range(lax.axis_size(axis))
    route = [((i - distance) % len(devices), i) for i in devices]
    return lax.ppermute(block, axis, route)


def beside_all(low_source, high_source, reach, sender):
    rows_here = low_source.shape[0]
    hop_count = (reach + rows_here - 1) // rows_here
    lower_parts = []
    upper_parts = []
    for distance in range(1, hop_count + 1):
        taken = min(rows_here, reach - rows_here * (distance - 1))
        lower_parts.insert(0, sender(low_source, distance))
        upper_parts.append(sender(high_source, -distance))
    return (jnp.concatenate(lower_parts, axis=0), jnp.concatenate(upper_parts, axis=0))


def passed(low_source, high_source, reach, send_low, send_high):
    rows_here = low_source.shape[0]
    hop_count = (reach + rows_here - 1) // rows_here
    first_keep = min(rows_here, reach)
    tail_blocks = low_source
    head_blocks = high_source
    from_low = tail_blocks
    from_high = head_blocks
    for hop_index in range(hop_count):
        from_low = send_low(tail_blocks)
        from_high = send_high(head_blocks)
        if hop_index + 1 < hop_count:
            keeping = min(reach, from_low.shape[0] + rows_here)
            joined_low = jnp.concatenate([from_low, low_source], axis=0)
            tail_blocks = joined_low
            joined_high = jnp.concatenate([high_source, from_high], axis=0)
            head_blocks = joined_high
    return (from_low, from_high)


def body(
    partner_aux_tiles,
    row_aux_tiles,
    tile_partner,
    tile_count,
    density_blocks,
    density_cols,
    density_count,
):
    n_row = lax.axis_size("row")
    my_row = lax.axis_index("row")
    rows_here = tile_count.shape[0]
    slots = tile_partner.shape[0] // rows_here
    dense_slots = density_cols.shape[0] // rows_here
    block_size = density_blocks.shape[1]
    aux_width = row_aux_tiles.shape[2] // block_size
    all_blocks = n_row * rows_here
    window = 2 * REACH + 1
    partner = tile_partner.reshape(rows_here, slots)
    dense_cols = density_cols.reshape(rows_here, dense_slots)
    active = jnp.arange(slots, dtype=jnp.int32)[None, :] < tile_count[:, None]
    dense_on = jnp.arange(dense_slots, dtype=jnp.int32)[None, :] < density_count[:, None]
    matches = (
        (partner[:, :, None] == dense_cols[:, None, :]) & active[:, :, None] & dense_on[:, None, :]
    )
    density = density_blocks.reshape(rows_here, dense_slots, block_size, block_size)
    selected = jnp.einsum(
        "buj,bjac->buac", matches.astype(jnp.bfloat16), density, preferred_element_type=jnp.float32
    ).astype(jnp.bfloat16)
    row_tiles = row_aux_tiles.reshape(rows_here, slots, block_size, block_size, aux_width)
    contracted = jnp.einsum(
        "buac,bukcp->bkap", selected, row_tiles, preferred_element_type=jnp.float32
    )
    contracted = contracted.reshape(rows_here, block_size, block_size * aux_width).astype(
        jnp.bfloat16
    )
    global_rows = my_row * rows_here + jnp.arange(rows_here, dtype=jnp.int32)
    offsets = (partner - global_rows[:, None] + REACH) % all_blocks - REACH
    relative = jnp.arange(window, dtype=jnp.int32) - REACH
    picked = ((offsets[:, :, None] == relative[None, None, :]) & active[:, :, None]).astype(
        jnp.bfloat16
    )
    pair_tiles = partner_aux_tiles.reshape(rows_here, slots, block_size, block_size * aux_width)
    chosen = jnp.einsum(
        "bts,btix->bsix", picked, pair_tiles, preferred_element_type=jnp.float32
    ).astype(jnp.bfloat16)
    lower_near, upper_near = passed(
        contracted,
        contracted,
        REACH,
        lambda blocks: passed_along(blocks, "row", 1),
        lambda blocks: passed_along(blocks, "row", -1),
    )
    extended = jnp.concatenate([lower_near, contracted, upper_near], axis=0)
    half_parts = []
    for column in range(window):
        half_parts.append(
            jnp.einsum(
                "bix,bkx->bik",
                chosen[:, column],
                extended[column : column + rows_here],
                preferred_element_type=jnp.float32,
            )
        )
    half_term = jnp.stack(half_parts, axis=2)
    low_source = half_term[:, :, REACH + 1 :, :]
    high_source = half_term[:, :, :REACH, :]
    lower_mirror, upper_mirror = beside_all(
        low_source, high_source, REACH, lambda blocks, steps: passed_along(blocks, "row", steps)
    )
    columns = []
    for column in range(window):
        offset_now = column - REACH
        if offset_now == 0:
            mirrored = half_term[:, :, REACH, :]
        elif offset_now > 0:
            component = REACH - offset_now
            joined = jnp.concatenate(
                [high_source[:, :, component, :], upper_mirror[:, :, component, :]], axis=0
            )
            mirrored = joined[offset_now : offset_now + rows_here]
        else:
            component = -offset_now - 1
            joined = jnp.concatenate(
                [lower_mirror[:, :, component, :], low_source[:, :, component, :]], axis=0
            )
            begin = REACH + offset_now
            mirrored = joined[begin : begin + rows_here]
        columns.append(half_term[:, :, column, :] + jnp.swapaxes(mirrored, 1, 2))
    return jnp.stack(columns, axis=2).reshape(rows_here * block_size, window * block_size)


def solution(mesh):
    in_specs = (
        P(("groups", "row"), None, None),
        P(("groups", "row"), None, None),
        P(("groups", "row")),
        P(("groups", "row")),
        P(("groups", "row"), None, None),
        P(("groups", "row")),
        P(("groups", "row")),
    )
    out_specs = P(("groups", "row"), None)
    return jax.shard_map(body, mesh=mesh, in_specs=in_specs, out_specs=out_specs, check_vma=False)
```

profile of v0, /device:TPU:5, one launch (start us, length us, event | category | flops | bytes accessed | tf_op | source)
XLA Modules:
  0.0 133.3 jit_solution(7725013628323487758)
XLA Ops:
  1.4 2.0 %copy.40 = bf16[8,64,1024]{1,2,0:T(8,128)(2,1)S(1)} copy(bf16[8,64,1024]{2,1,0:T(8,128)(2,1)} %param.8) | data formatting | bytes 2097152 | tf_op args[1]
  4.4 0.7 collective-permute-start.5
  5.2 2.0 %collective-permute-start = (bf16[1,64,1024]{1,2,0:T(8,128)(2,1)S(1)}, bf16[1,64,1024]{1,2,0:T(8,128)(2,1)S(1)}, u32[]{:S(2)}, u32[]{:S(2)}) collective-permute-start(bf16[1,64,1024]{1,2,0:T(8,128)(2,1)S(1)} %bitcast.328), channel_id=1, source_target_pairs={{15,0},{0,1},{1,2},{2,3},{3,4},{4,5},{5,6},{6,7},{7,8},{8,9},{9,10... | collective-permute-start | bytes 393224 | tf_op jit(solution)/shard_map/ppermute | solution.py:12
  7.1 4.2 %collective-permute-done.5 = bf16[1,64,1024]{1,2,0:T(8,128)(2,1)S(1)} collective-permute-done((bf16[1,64,1024]{1,2,0:T(8,128)(2,1)S(1)}, bf16[1,64,1024]{1,2,0:T(8,128)(2,1)S(1)}, u32[]{:S(2)}, u32[]{:S(2)}) %collective-permute-start.5) | collective-permute-done | bytes 131104 | tf_op jit(solution)/shard_map/ppermute | solution.py:12
  11.5 2.6 %collective-permute-start.6 = (bf16[2,64,1024]{1,2,0:T(8,128)(2,1)S(1)}, bf16[2,64,1024]{1,2,0:T(8,128)(2,1)S(1)}, u32[]{:S(2)}, u32[]{:S(2)}) collective-permute-start(bf16[2,64,1024]{1,2,0:T(8,128)(2,1)S(1)} %get-tuple-element.18), channel_id=1, source_target_pairs={{1,0},{2,1},{3,2},{4,3},{5,4},{6,5},{7,6},{8,7},{9,8},{10,9},{11,1... | collective-permute-start | bytes 786440 | tf_op jit(solution)/shard_map/ppermute | solution.py:12
  14.3 6.9 %collective-permute-done.6 = bf16[2,64,1024]{1,2,0:T(8,128)(2,1)S(1)} collective-permute-done((bf16[2,64,1024]{1,2,0:T(8,128)(2,1)S(1)}, bf16[2,64,1024]{1,2,0:T(8,128)(2,1)S(1)}, u32[]{:S(2)}, u32[]{:S(2)}) %collective-permute-start.6) | collective-permute-done | bytes 262176 | tf_op jit(solution)/shard_map/ppermute | solution.py:12
  22.1 2.8 %collective-permute-start.2 = (bf16[3,64,1024]{2,1,0:T(8,128)(2,1)S(1)}, bf16[3,64,1024]{2,1,0:T(8,128)(2,1)S(1)}, u32[]{:S(2)}, u32[]{:S(2)}) collective-permute-start(bf16[3,64,1024]{2,1,0:T(8,128)(2,1)S(1)} %copy.44), channel_id=1, source_target_pairs={{15,0},{0,1},{1,2},{2,3},{3,4},{4,5},{5,6},{6,7},{7,8},{8,9},{9,10... | collective-permute-start | bytes 1179656 | tf_op jit(solution)/shard_map/ppermute | solution.py:12
  24.8 3.6 %collective-permute-start.7 = (bf16[3,64,1024]{2,1,0:T(8,128)(2,1)S(1)}, bf16[3,64,1024]{2,1,0:T(8,128)(2,1)}, u32[]{:S(2)}, u32[]{:S(2)}) collective-permute-start(bf16[3,64,1024]{2,1,0:T(8,128)(2,1)S(1)} %copy.47), channel_id=1, source_target_pairs={{1,0},{2,1},{3,2},{4,3},{5,4},{6,5},{7,6},{8,7},{9,8},{10,9},{11,1... | collective-permute-start | bytes 1179656 | tf_op jit(solution)/shard_map/ppermute | solution.py:12
  28.5 1.1 collective-permute-done.2
  29.6 10.3 %collective-permute-done.7 = bf16[3,64,1024]{2,1,0:T(8,128)(2,1)} collective-permute-done((bf16[3,64,1024]{2,1,0:T(8,128)(2,1)S(1)}, bf16[3,64,1024]{2,1,0:T(8,128)(2,1)}, u32[]{:S(2)}, u32[]{:S(2)}) %collective-permute-start.7) | collective-permute-done | bytes 393248 | tf_op jit(solution)/shard_map/ppermute | solution.py:12
  39.9 1.1 pad_maximum_fusion.7
  41.1 2.6 %collective-permute-start.3 = (bf16[4,64,1024]{2,1,0:T(8,128)(2,1)S(1)}, bf16[4,64,1024]{2,1,0:T(8,128)(2,1)}, u32[]{:S(2)}, u32[]{:S(2)}) collective-permute-start(bf16[4,64,1024]{2,1,0:T(8,128)(2,1)S(1)} %get-tuple-element.23), channel_id=1, source_target_pairs={{15,0},{0,1},{1,2},{2,3},{3,4},{4,5},{5,6},{6,7},{7,8},{8,9},{9,10... | collective-permute-start | bytes 1572872 | tf_op jit(solution)/shard_map/ppermute | solution.py:12
  43.7 0.9 convert_bitcast_fusion
  44.7 6.0 %collective-permute-done.8 = bf16[4,64,1024]{2,1,0:T(8,128)(2,1)S(1)} collective-permute-done((bf16[4,64,1024]{2,1,0:T(8,128)(2,1)S(1)}, bf16[4,64,1024]{2,1,0:T(8,128)(2,1)S(1)}, u32[]{:S(2)}, u32[]{:S(2)}) %collective-permute-start.8) | collective-permute-done | bytes 524320 | tf_op jit(solution)/shard_map/ppermute | solution.py:12
  50.7 1.2 pad_maximum_fusion.3
  51.8 13.4 %collective-permute-start.9 = (bf16[5,64,1024]{2,1,0:T(8,128)(2,1)S(1)}, bf16[5,64,1024]{2,1,0:T(8,128)(2,1)}, u32[]{:S(2)}, u32[]{:S(2)}) collective-permute-start(bf16[5,64,1024]{2,1,0:T(8,128)(2,1)S(1)} %get-tuple-element.20), channel_id=1, source_target_pairs={{1,0},{2,1},{3,2},{4,3},{5,4},{6,5},{7,6},{8,7},{9,8},{10,9},{11,1... | collective-permute-start | bytes 1966088 | tf_op jit(solution)/shard_map/ppermute | solution.py:12
  65.2 3.1 %fusion.85 = (bf16[1,1,64,1024]{3,1,2,0:T(2,128)(2,1)S(1)}, bf16[1,1,64,1024]{3,1,2,0:T(2,128)(2,1)S(1)}, bf16[1,1,64,1024]{3,1,2,0:T(2,128)(2,1)S(1)}, bf16[1,1...) fusion(bf16[1,11,64,1024]{3,1,2,0:T(8,128)(2,1)S(1)} %convert_b, ...), kind=kLoop, calls=%fused_computation.137 | loop fusion | bytes 2883584 | tf_op jit(solution)/shard_map/slice | solution.py:106
  68.5 0.7 copy.56
  69.3 1.8 %constant_dynamic-update-slice_fusion.4 = (f32[1,64,5,64]{3,1,2,0:T(8,128)}, f32[64,64]{1,0:T(8,128)S(1)}) fusion(bf16[5,64,1024]{2,1,0:T(8,128)(2,1)} %collective-permute-done.9, bf16[1,1,64,1024]{3,1,2,0:T(2,128)(2,1)} %get-tuple-element.14), kind=kOutput, calls=%fused_computation.66 | convolution fusion | flops 8388607 | bytes 442368 | tf_op jit(solution)/shard_map/bix,bkx->bik/dot_general | solution.py:104
  71.0 1.8 %constant_dynamic-update-slice_fusion.3 = (f32[1,64,5,64]{3,1,2,0:T(8,128)}, f32[64,64]{1,0:T(8,128)S(1)}) fusion(f32[1,64,5,64]{3,1,2,0:T(8,128)} %get-tuple-element.24, bf16[5,64,1024]{2,1,0:T(8,128)(2,1)} %collective-permute-done.9, bf16[1,1,64,1024]{3,1,2,0:T(2,128)(2,1)} %get-tuple-element.13), kind=kOutput, calls=%fused_computation.65 | convolution fusion | flops 8388608 | bytes 442368 | tf_op jit(solution)/shard_map/bix,bkx->bik/dot_general | solution.py:104
  72.8 1.8 %constant_dynamic-update-slice_fusion.2 = (f32[1,64,5,64]{3,1,2,0:T(8,128)}, f32[64,64]{1,0:T(8,128)S(1)}) fusion(f32[1,64,5,64]{3,1,2,0:T(8,128)} %get-tuple-element.26, bf16[5,64,1024]{2,1,0:T(8,128)(2,1)} %collective-permute-done.9, bf16[1,1,64,1024]{3,1,2,0:T(2,128)(2,1)} %get-tuple-element.12), kind=kOutput, calls=%fused_computation.64 | convolution fusion | flops 8388608 | bytes 442368 | tf_op jit(solution)/shard_map/bix,bkx->bik/dot_general | solution.py:104
  74.6 1.8 %constant_dynamic-update-slice_fusion.1 = (f32[1,64,5,64]{3,1,2,0:T(8,128)}, f32[64,64]{1,0:T(8,128)S(1)}) fusion(f32[1,64,5,64]{3,1,2,0:T(8,128)} %get-tuple-element.28, bf16[5,64,1024]{2,1,0:T(8,128)(2,1)} %collective-permute-done.9, bf16[1,1,64,1024]{3,1,2,0:T(2,128)(2,1)} %get-tuple-element.11), kind=kOutput, calls=%fused_computation.63 | convolution fusion | flops 8388608 | bytes 442368 | tf_op jit(solution)/shard_map/bix,bkx->bik/dot_general | solution.py:104
  76.4 1.8 %constant_dynamic-update-slice_fusion = (f32[1,64,5,64]{3,1,2,0:T(8,128)}, f32[64,64]{1,0:T(8,128)S(1)}) fusion(f32[1,64,5,64]{3,1,2,0:T(8,128)} %get-tuple-element.30, bf16[5,64,1024]{2,1,0:T(8,128)(2,1)} %collective-permute-done.9, bf16[1,1,64,1024]{3,1,2,0:T(2,128)(2,1)} %get-tuple-element.10), kind=kOutput, calls=%fused_computation.62 | convolution fusion | flops 8388608 | bytes 442368 | tf_op jit(solution)/shard_map/bix,bkx->bik/dot_general | solution.py:104
  78.5 11.3 %collective-permute-start.12 = (f32[1,64,5,64]{3,1,2,0:T(8,128)}, f32[1,64,5,64]{3,1,2,0:T(8,128)S(1)}, u32[]{:S(2)}, u32[]{:S(2)}) collective-permute-start(f32[1,64,5,64]{3,1,2,0:T(8,128)} %get-tuple-element.32), channel_id=1, source_target_pairs={{13,0},{14,1},{15,2},{0,3},{1,4},{2,5},{3,6},{4,7},{5,8},{6,9},{7,... | collective-permute-start | bytes 245768 | tf_op jit(solution)/shard_map/ppermute | solution.py:12
  89.8 1.7 %collective-permute-start.11 = (f32[1,64,5,64]{3,1,2,0:T(8,128)}, f32[1,64,5,64]{3,1,2,0:T(8,128)}, u32[]{:S(2)}, u32[]{:S(2)}) collective-permute-start(f32[1,64,5,64]{3,1,2,0:T(8,128)} %get-tuple-element.32), channel_id=1, source_target_pairs={{12,0},{13,1},{14,2},{15,3},{0,4},{1,5},{2,6},{3,7},{4,8},{5,9},{6... | collective-permute-start | bytes 245768 | tf_op jit(solution)/shard_map/ppermute | solution.py:12
  91.5 6.2 %collective-permute-start.10 = (f32[1,64,5,64]{3,1,2,0:T(8,128)}, f32[1,64,5,64]{3,1,2,0:T(8,128)S(1)}, u32[]{:S(2)}, u32[]{:S(2)}) collective-permute-start(f32[1,64,5,64]{3,1,2,0:T(8,128)} %get-tuple-element.32), channel_id=1, source_target_pairs={{11,0},{12,1},{13,2},{14,3},{15,4},{0,5},{1,6},{2,7},{3,8},{4,9},{... | collective-permute-start | bytes 245768 | tf_op jit(solution)/shard_map/ppermute | solution.py:12
  97.6 1.1 constant_dynamic-update-slice_fusion.9
  101.0 10.0 %collective-permute-done.10 = f32[1,64,5,64]{3,1,2,0:T(8,128)S(1)} collective-permute-done((f32[1,64,5,64]{3,1,2,0:T(8,128)}, f32[1,64,5,64]{3,1,2,0:T(8,128)S(1)}, u32[]{:S(2)}, u32[]{:S(2)}) %collective-permute-start.10) | collective-permute-done | bytes 81952 | tf_op jit(solution)/shard_map/ppermute | solution.py:12
  111.1 0.8 constant_dynamic-update-slice_fusion.19
  111.9 5.0 %collective-permute-start.17 = (f32[1,64,5,64]{3,1,2,0:T(8,128)}, f32[1,64,5,64]{3,1,2,0:T(8,128)S(1)}, u32[]{:S(2)}, u32[]{:S(2)}) collective-permute-start(f32[1,64,5,64]{3,1,2,0:T(8,128)} %copy-done.6), channel_id=1, source_target_pairs={{3,0},{4,1},{5,2},{6,3},{7,4},{8,5},{9,6},{10,7},{11,8},{12,9},{13... | collective-permute-start | bytes 245768 | tf_op jit(solution)/shard_map/ppermute | solution.py:12
  117.4 15.0 %collective-permute-done.15 = f32[1,64,5,64]{3,1,2,0:T(8,128)S(1)} collective-permute-done((f32[1,64,5,64]{3,1,2,0:T(8,128)}, f32[1,64,5,64]{3,1,2,0:T(8,128)S(1)}, u32[]{:S(2)}, u32[]{:S(2)}) %collective-permute-start.15) | collective-permute-done | bytes 81952 | tf_op jit(solution)/shard_map/ppermute | solution.py:12
  132.5 0.8 copy.62
  (72 shorter events, 5.8 us)
Async XLA Ops:
  0.0 43.7 %copy-start = (bf16[8,64,1024]{2,1,0:T(8,128)(2,1)S(1)}, bf16[8,64,1024]{2,1,0:T(8,128)(2,1)}, u32[]{:S(2)}) copy-start(bf16[8,64,1024]{2,1,0:T(8,128)(2,1)} %param.7) | copy-start | bytes 3145732
  0.0 3.5 %copy-start.5 = (s32[8]{0:T(128)S(1)}, s32[8]{0:T(128)}, u32[]{:S(2)}) copy-start(s32[8]{0:T(128)} %param.9) | copy-start | bytes 100
  0.0 3.5 %copy-start.4 = (s32[8]{0:T(128)S(1)}, s32[8]{0:T(128)}, u32[]{:S(2)}) copy-start(s32[8]{0:T(128)} %param.12) | copy-start | bytes 100
  0.0 3.5 %copy-start.3 = (bf16[8,64,64]{2,1,0:T(8,128)(2,1)S(1)}, bf16[8,64,64]{2,1,0:T(8,128)(2,1)}, u32[]{:S(2)}) copy-start(bf16[8,64,64]{2,1,0:T(8,128)(2,1)} %param.11) | copy-start | bytes 196612
  4.4 6.9 %collective-permute-start.5 = (bf16[1,64,1024]{1,2,0:T(8,128)(2,1)S(1)}, bf16[1,64,1024]{1,2,0:T(8,128)(2,1)S(1)}, u32[]{:S(2)}, u32[]{:S(2)}) collective-permute-start(bf16[1,64,1024]{1,2,0:T(8,128)(2,1)S(1)} %bitcast.327), channel_id=1, source_target_pairs={{1,0},{2,1},{3,2},{4,3},{5,4},{6,5},{7,6},{8,7},{9,8},{10,9},{11,1... | collective-permute-start | bytes 393224 | tf_op jit(solution)/shard_map/ppermute | solution.py:12
  5.2 6.1 %collective-permute-start = (bf16[1,64,1024]{1,2,0:T(8,128)(2,1)S(1)}, bf16[1,64,1024]{1,2,0:T(8,128)(2,1)S(1)}, u32[]{:S(2)}, u32[]{:S(2)}) collective-permute-start(bf16[1,64,1024]{1,2,0:T(8,128)(2,1)S(1)} %bitcast.328), channel_id=1, source_target_pairs={{15,0},{0,1},{1,2},{2,3},{3,4},{4,5},{5,6},{6,7},{7,8},{8,9},{9,10... | collective-permute-start | bytes 393224 | tf_op jit(solution)/shard_map/ppermute | solution.py:12
  11.5 9.7 %collective-permute-start.6 = (bf16[2,64,1024]{1,2,0:T(8,128)(2,1)S(1)}, bf16[2,64,1024]{1,2,0:T(8,128)(2,1)S(1)}, u32[]{:S(2)}, u32[]{:S(2)}) collective-permute-start(bf16[2,64,1024]{1,2,0:T(8,128)(2,1)S(1)} %get-tuple-element.18), channel_id=1, source_target_pairs={{1,0},{2,1},{3,2},{4,3},{5,4},{6,5},{7,6},{8,7},{9,8},{10,9},{11,1... | collective-permute-start | bytes 786440 | tf_op jit(solution)/shard_map/ppermute | solution.py:12
  14.1 7.1 %collective-permute-start.1 = (bf16[2,64,1024]{1,2,0:T(8,128)(2,1)S(1)}, bf16[2,64,1024]{1,2,0:T(8,128)(2,1)S(1)}, u32[]{:S(2)}, u32[]{:S(2)}) collective-permute-start(bf16[2,64,1024]{1,2,0:T(8,128)(2,1)S(1)} %get-tuple-element.19), channel_id=1, source_target_pairs={{15,0},{0,1},{1,2},{2,3},{3,4},{4,5},{5,6},{6,7},{7,8},{8,9},{9,10... | collective-permute-start | bytes 786440 | tf_op jit(solution)/shard_map/ppermute | solution.py:12
  22.1 7.5 %collective-permute-start.2 = (bf16[3,64,1024]{2,1,0:T(8,128)(2,1)S(1)}, bf16[3,64,1024]{2,1,0:T(8,128)(2,1)S(1)}, u32[]{:S(2)}, u32[]{:S(2)}) collective-permute-start(bf16[3,64,1024]{2,1,0:T(8,128)(2,1)S(1)} %copy.44), channel_id=1, source_target_pairs={{15,0},{0,1},{1,2},{2,3},{3,4},{4,5},{5,6},{6,7},{7,8},{8,9},{9,10... | collective-permute-start | bytes 1179656 | tf_op jit(solution)/shard_map/ppermute | solution.py:12
  24.8 15.1 %collective-permute-start.7 = (bf16[3,64,1024]{2,1,0:T(8,128)(2,1)S(1)}, bf16[3,64,1024]{2,1,0:T(8,128)(2,1)}, u32[]{:S(2)}, u32[]{:S(2)}) collective-permute-start(bf16[3,64,1024]{2,1,0:T(8,128)(2,1)S(1)} %copy.47), channel_id=1, source_target_pairs={{1,0},{2,1},{3,2},{4,3},{5,4},{6,5},{7,6},{8,7},{9,8},{10,9},{11,1... | collective-permute-start | bytes 1179656 | tf_op jit(solution)/shard_map/ppermute | solution.py:12
  41.0 9.7 %collective-permute-start.8 = (bf16[4,64,1024]{2,1,0:T(8,128)(2,1)S(1)}, bf16[4,64,1024]{2,1,0:T(8,128)(2,1)S(1)}, u32[]{:S(2)}, u32[]{:S(2)}) collective-permute-start(bf16[4,64,1024]{2,1,0:T(8,128)(2,1)S(1)} %get-tuple-element.22), channel_id=1, source_target_pairs={{1,0},{2,1},{3,2},{4,3},{5,4},{6,5},{7,6},{8,7},{9,8},{10,9},{11,1... | collective-permute-start | bytes 1572872 | tf_op jit(solution)/shard_map/ppermute | solution.py:12
  41.1 9.6 %collective-permute-start.3 = (bf16[4,64,1024]{2,1,0:T(8,128)(2,1)S(1)}, bf16[4,64,1024]{2,1,0:T(8,128)(2,1)}, u32[]{:S(2)}, u32[]{:S(2)}) collective-permute-start(bf16[4,64,1024]{2,1,0:T(8,128)(2,1)S(1)} %get-tuple-element.23), channel_id=1, source_target_pairs={{15,0},{0,1},{1,2},{2,3},{3,4},{4,5},{5,6},{6,7},{7,8},{8,9},{9,10... | collective-permute-start | bytes 1572872 | tf_op jit(solution)/shard_map/ppermute | solution.py:12
  51.8 17.4 %collective-permute-start.9 = (bf16[5,64,1024]{2,1,0:T(8,128)(2,1)S(1)}, bf16[5,64,1024]{2,1,0:T(8,128)(2,1)}, u32[]{:S(2)}, u32[]{:S(2)}) collective-permute-start(bf16[5,64,1024]{2,1,0:T(8,128)(2,1)S(1)} %get-tuple-element.20), channel_id=1, source_target_pairs={{1,0},{2,1},{3,2},{4,3},{5,4},{6,5},{7,6},{8,7},{9,8},{10,9},{11,1... | collective-permute-start | bytes 1966088 | tf_op jit(solution)/shard_map/ppermute | solution.py:12
  68.5 30.2 %copy-start.1 = (bf16[1,1,64,1024]{3,1,2,0:T(2,128)(2,1)S(1)}, bf16[1,1,64,1024]{3,1,2,0:T(2,128)(2,1)}, u32[]{:S(2)}) copy-start(bf16[1,1,64,1024]{3,1,2,0:T(2,128)(2,1)} %get-tuple-element.9) | copy-start | bytes 393220
  69.2 22.2 %collective-permute-start.4 = (bf16[5,64,1024]{2,1,0:T(8,128)(2,1)S(1)}, bf16[5,64,1024]{2,1,0:T(8,128)(2,1)S(1)}, u32[]{:S(2)}, u32[]{:S(2)}) collective-permute-start(bf16[5,64,1024]{2,1,0:T(8,128)(2,1)S(1)} %get-tuple-element.21), channel_id=1, source_target_pairs={{15,0},{0,1},{1,2},{2,3},{3,4},{4,5},{5,6},{6,7},{7,8},{8,9},{9,10... | collective-permute-start | bytes 1966088 | tf_op jit(solution)/shard_map/ppermute | solution.py:12
  71.0 46.4 %copy-start.2 = (f32[1,64,64]{1,2,0:T(8,128)S(1)}, f32[1,64,64]{1,2,0:T(8,128)}, u32[]{:S(2)}) copy-start(f32[1,64,64]{1,2,0:T(8,128)} %copy.56) | copy-start | bytes 49156
  78.1 38.8 %collective-permute-start.14 = (f32[1,64,5,64]{3,1,2,0:T(8,128)}, f32[1,64,5,64]{3,1,2,0:T(8,128)S(1)}, u32[]{:S(2)}, u32[]{:S(2)}) collective-permute-start(f32[1,64,5,64]{3,1,2,0:T(8,128)} %get-tuple-element.32), channel_id=1, source_target_pairs={{15,0},{0,1},{1,2},{2,3},{3,4},{4,5},{5,6},{6,7},{7,8},{8,9},{9,10... | collective-permute-start | bytes 245768 | tf_op jit(solution)/shard_map/ppermute | solution.py:12
  78.1 38.7 %collective-permute-start.13 = (f32[1,64,5,64]{3,1,2,0:T(8,128)}, f32[1,64,5,64]{3,1,2,0:T(8,128)S(1)}, u32[]{:S(2)}, u32[]{:S(2)}) collective-permute-start(f32[1,64,5,64]{3,1,2,0:T(8,128)} %get-tuple-element.32), channel_id=1, source_target_pairs={{14,0},{15,1},{0,2},{1,3},{2,4},{3,5},{4,6},{5,7},{6,8},{7,9},{8,1... | collective-permute-start | bytes 245768 | tf_op jit(solution)/shard_map/ppermute | solution.py:12
  78.5 33.4 %collective-permute-start.12 = (f32[1,64,5,64]{3,1,2,0:T(8,128)}, f32[1,64,5,64]{3,1,2,0:T(8,128)S(1)}, u32[]{:S(2)}, u32[]{:S(2)}) collective-permute-start(f32[1,64,5,64]{3,1,2,0:T(8,128)} %get-tuple-element.32), channel_id=1, source_target_pairs={{13,0},{14,1},{15,2},{0,3},{1,4},{2,5},{3,6},{4,7},{5,8},{6,9},{7,... | collective-permute-start | bytes 245768 | tf_op jit(solution)/shard_map/ppermute | solution.py:12
  89.8 21.2 %collective-permute-start.11 = (f32[1,64,5,64]{3,1,2,0:T(8,128)}, f32[1,64,5,64]{3,1,2,0:T(8,128)}, u32[]{:S(2)}, u32[]{:S(2)}) collective-permute-start(f32[1,64,5,64]{3,1,2,0:T(8,128)} %get-tuple-element.32), channel_id=1, source_target_pairs={{12,0},{13,1},{14,2},{15,3},{0,4},{1,5},{2,6},{3,7},{4,8},{5,9},{6... | collective-permute-start | bytes 245768 | tf_op jit(solution)/shard_map/ppermute | solution.py:12
  91.5 19.5 %collective-permute-start.10 = (f32[1,64,5,64]{3,1,2,0:T(8,128)}, f32[1,64,5,64]{3,1,2,0:T(8,128)S(1)}, u32[]{:S(2)}, u32[]{:S(2)}) collective-permute-start(f32[1,64,5,64]{3,1,2,0:T(8,128)} %get-tuple-element.32), channel_id=1, source_target_pairs={{11,0},{12,1},{13,2},{14,3},{15,4},{0,5},{1,6},{2,7},{3,8},{4,9},{... | collective-permute-start | bytes 245768 | tf_op jit(solution)/shard_map/ppermute | solution.py:12
  99.5 0.7 copy-start.6
  111.0 21.5 %collective-permute-start.19 = (f32[1,64,5,64]{3,1,2,0:T(8,128)}, f32[1,64,5,64]{3,1,2,0:T(8,128)S(1)}, u32[]{:S(2)}, u32[]{:S(2)}) collective-permute-start(f32[1,64,5,64]{3,1,2,0:T(8,128)} %copy-done.6), channel_id=1, source_target_pairs={{5,0},{6,1},{7,2},{8,3},{9,4},{10,5},{11,6},{12,7},{13,8},{14,9},{... | collective-permute-start | bytes 245768 | tf_op jit(solution)/shard_map/ppermute | solution.py:12
  111.0 21.4 %collective-permute-start.18 = (f32[1,64,5,64]{3,1,2,0:T(8,128)}, f32[1,64,5,64]{3,1,2,0:T(8,128)S(1)}, u32[]{:S(2)}, u32[]{:S(2)}) collective-permute-start(f32[1,64,5,64]{3,1,2,0:T(8,128)} %copy-done.6), channel_id=1, source_target_pairs={{4,0},{5,1},{6,2},{7,3},{8,4},{9,5},{10,6},{11,7},{12,8},{13,9},{1... | collective-permute-start | bytes 245768 | tf_op jit(solution)/shard_map/ppermute | solution.py:12
  111.9 20.6 %collective-permute-start.17 = (f32[1,64,5,64]{3,1,2,0:T(8,128)}, f32[1,64,5,64]{3,1,2,0:T(8,128)S(1)}, u32[]{:S(2)}, u32[]{:S(2)}) collective-permute-start(f32[1,64,5,64]{3,1,2,0:T(8,128)} %copy-done.6), channel_id=1, source_target_pairs={{3,0},{4,1},{5,2},{6,3},{7,4},{8,5},{9,6},{10,7},{11,8},{12,9},{13... | collective-permute-start | bytes 245768 | tf_op jit(solution)/shard_map/ppermute | solution.py:12
  116.9 15.5 %collective-permute-start.16 = (f32[1,64,5,64]{3,1,2,0:T(8,128)}, f32[1,64,5,64]{3,1,2,0:T(8,128)S(1)}, u32[]{:S(2)}, u32[]{:S(2)}) collective-permute-start(f32[1,64,5,64]{3,1,2,0:T(8,128)} %copy-done.6), channel_id=1, source_target_pairs={{2,0},{3,1},{4,2},{5,3},{6,4},{7,5},{8,6},{9,7},{10,8},{11,9},{12,... | collective-permute-start | bytes 245768 | tf_op jit(solution)/shard_map/ppermute | solution.py:12
  117.0 15.4 %collective-permute-start.15 = (f32[1,64,5,64]{3,1,2,0:T(8,128)}, f32[1,64,5,64]{3,1,2,0:T(8,128)S(1)}, u32[]{:S(2)}, u32[]{:S(2)}) collective-permute-start(f32[1,64,5,64]{3,1,2,0:T(8,128)} %copy-done.6), channel_id=1, source_target_pairs={{1,0},{2,1},{3,2},{4,3},{5,4},{6,5},{7,6},{8,7},{9,8},{10,9},{11,1... | collective-permute-start | bytes 245768 | tf_op jit(solution)/shard_map/ppermute | solution.py:12
where the time goes:
time: 134 us; the launch traced here: 133 us
  waiting for transfers between devices  53.5 us (40%)
  starting transfers between devices  52.9 us (39%)
  matrix products  12.5 us (9%)
  local copies, waits for them, and re-layouts  9.02 us (7%)
  other arithmetic  3.64 us (3%)
  between operations  1.72 us (1%)
    ppermute x20, waiting for transfers between devices, passed_along(): return lax.ppermute(block, axis, route)  53.5 us
    ppermute x20, starting transfers between devices, passed_along(): return lax.ppermute(block, axis, route)  52.9 us
    dot_general x11, matrix products, body(): jnp.einsum('bix,bkx->bik', chosen[:, column], extended[column:column + ro...  10.9 us
    slice x1, local copies, waits for them, and re-layouts, body(): chosen[:, column]  3.14 us
    concatenate x4, other arithmetic, passed(): joined_high = jnp.concatenate([high_source, from_high], axis=0)  2.79 us
    unnamed x15, local copies, waits for them, and re-layouts  2.71 us
  transfers between devices with their start and end apart: 20, of which 7 were waited for; matrix products, arithmetic and copies ran while one was open for 13% of the time, Pallas kernels for 0%

commit v1 on v0

v1 whole, which is shorter than its diff:
```python
import functools

import jax
import jax.numpy as jnp
from jax import lax
from jax.experimental import pallas as pl
from jax.experimental.pallas import tpu as pltpu
from jax.sharding import PartitionSpec as P

REACH = 5
CHUNKS = 2
DIRECT = (2, -2, 4, -4)
N_T = (((1,), (1,)), ((), ()))


def kernel(n, row_hbm, pair_hbm, partner, count, density, cols, dense_count, out,
           row_v, pair_v, perm, row_p, pair_p, weights, mine, near, half, leaving, mirror,
           load_sem, send_sem, pass_sem, near_sem, back_sem, mirror_sem):
    slots, blk, width = row_v.shape
    dense = density.shape[0]
    aux = width // blk
    group = 256
    n_group = width // group
    per_chunk = n_group // CHUNKS
    span = width // CHUNKS

    me = lax.axis_index("row")
    core = lax.rem(me, 2)
    side = 1 - 2 * core

    def at(offset):
        return {"row": lax.rem(me + offset + n, n)}

    load_row = pltpu.make_async_copy(row_hbm, row_v, load_sem.at[0])
    load_pair = pltpu.make_async_copy(pair_hbm, pair_v, load_sem.at[1])
    load_row.start()
    load_pair.start()
    barrier = pltpu.get_barrier_semaphore()
    for offset in range(-REACH, REACH + 1):
        if offset:
            pl.semaphore_signal(barrier, inc=1, device_id=at(offset),
                                device_id_type=pl.DeviceIdType.MESH)

    x = lax.broadcasted_iota(jnp.int32, (width, 128), 0)
    goes_to = lax.div(x, aux) + lax.rem(x, aux) * blk
    lane = lax.broadcasted_iota(jnp.int32, (width, 128), 1)
    for tile in range(width // 128):
        perm[:, tile * 128:(tile + 1) * 128] = jnp.where(
            goes_to == lane + tile * 128, 1.0, 0.0).astype(jnp.bfloat16)

    live_tiles = count[0]
    live_dense = dense_count[0]
    zero = jnp.zeros((blk, blk), jnp.bfloat16)
    wide_zero = jnp.zeros((2 * blk, 2 * blk), jnp.bfloat16)
    for u in range(slots):
        index = jnp.int32(0)
        found = jnp.int32(0)
        for j in range(dense):
            hit = ((cols[j] == partner[u]) & (j < live_dense)).astype(jnp.int32)
            index += hit * j
            found += hit
        found *= (u < live_tiles).astype(jnp.int32)
        d = (density[index].astype(jnp.float32) * found.astype(jnp.float32)).astype(jnp.bfloat16)
        left = jnp.concatenate([d, zero], axis=1)
        right = jnp.concatenate([zero, d], axis=1)
        weights[u, 0:64, 0:128] = left
        weights[u, 64:128, 0:128] = right
        weights[u, 128:192, 128:256] = left
        weights[u, 192:256, 128:256] = right
        weights[u, 0:128, 128:256] = wide_zero
        weights[u, 128:256, 0:128] = wide_zero

    def reorder(source, target, g):
        flat = source[...].reshape(slots * blk, width)
        part = jnp.dot(flat, perm[:, g * group:(g + 1) * group],
                       preferred_element_type=jnp.float32)
        target[:, :, g * group:(g + 1) * group] = part.astype(jnp.bfloat16).reshape(
            slots, blk, group)

    sends = []
    load_row.wait()
    for h in range(CHUNKS):
        for step in range(per_chunk):
            g = h * per_chunk + step
            reorder(row_v, row_p, g)
            total = jnp.zeros((blk, group), jnp.float32)
            for u in range(slots):
                total += lax.dot_general(row_p[u, :, g * group:(g + 1) * group], weights[u], N_T,
                                         preferred_element_type=jnp.float32)
            mine[h, :, step * group:(step + 1) * group] = total.astype(jnp.bfloat16)
        if h == 0:
            pl.semaphore_wait(barrier, 2 * REACH)
        for slot, offset in ((0, -2), (1, 2), (2, -4), (3, 4), (4, side), (9, -5 * side)):
            number = slot if slot < 5 else 5
            copy = pltpu.make_async_remote_copy(
                src_ref=mine.at[h], dst_ref=near.at[slot, h],
                send_sem=send_sem.at[number, h], recv_sem=near_sem.at[slot, h],
                device_id=at(offset), device_id_type=pl.DeviceIdType.MESH)
            copy.start()
            sends.append(copy)

    def arrived(slot, h):
        pltpu.make_async_remote_copy(
            src_ref=mine.at[h], dst_ref=near.at[slot, h],
            send_sem=send_sem.at[0, h], recv_sem=near_sem.at[slot, h],
            device_id=at(side), device_id_type=pl.DeviceIdType.MESH).wait_recv()

    load_pair.wait()
    for g in range(n_group):
        reorder(pair_v, pair_p, g)

    where = [lax.rem(partner[t] - me + REACH + n, n) - REACH for t in range(slots)]

    def term(offset, block):
        index = jnp.int32(0)
        found = jnp.int32(0)
        for t in range(slots):
            hit = ((where[t] == offset) & (t < live_tiles)).astype(jnp.int32)
            index += hit * t
            found += hit
        total = jnp.zeros((blk, blk), jnp.float32)
        for h in range(CHUNKS):
            total += lax.dot_general(pair_p[index, :, h * span:(h + 1) * span], block(h), N_T,
                                     preferred_element_type=jnp.float32)
        return total * found.astype(jnp.float32)

    own = term(0, lambda h: mine[h])
    half[REACH] = own + own.T

    for h in range(CHUNKS):
        for slot in range(4):
            arrived(slot, h)
            copy = pltpu.make_async_remote_copy(
                src_ref=near.at[slot, h], dst_ref=near.at[5 + slot, h],
                send_sem=pass_sem.at[slot, h], recv_sem=near_sem.at[5 + slot, h],
                device_id=at(side), device_id_type=pl.DeviceIdType.MESH)
            copy.start()
            sends.append(copy)

    order = [(4, side), (0, 2), (1, -2), (5, 2 + side), (6, -2 + side), (2, 4), (3, -4),
             (7, 4 + side), (8, -4 + side), (9, -5 * side)]
    for slot, offset in order:
        if slot >= 4:
            for h in range(CHUNKS):
                arrived(slot, h)
        value = term(offset, lambda h: near[slot, h])
        half[REACH + offset] = value
        turned = value.T
        leaving[slot] = jnp.concatenate([turned[:blk // 2], turned[blk // 2:]], axis=1)
        copy = pltpu.make_async_remote_copy(
            src_ref=leaving.at[slot], dst_ref=mirror.at[REACH - offset],
            send_sem=back_sem.at[slot], recv_sem=mirror_sem.at[REACH - offset],
            device_id=at(offset), device_id_type=pl.DeviceIdType.MESH)
        copy.start()
        sends.append(copy)

    for s in range(2 * REACH + 1):
        value = half[s]
        if s != REACH:
            pltpu.make_async_remote_copy(
                src_ref=leaving.at[0], dst_ref=mirror.at[s],
                send_sem=back_sem.at[0], recv_sem=mirror_sem.at[s],
                device_id=at(side), device_id_type=pl.DeviceIdType.MESH).wait_recv()
            other = mirror[s]
            value += jnp.concatenate([other[:, :blk], other[:, blk:]], axis=0)
        out[:, s * blk:(s + 1) * blk] = value
    for copy in sends:
        copy.wait_send()


def body(partner_aux_tiles, row_aux_tiles, tile_partner, tile_count, density_blocks,
         density_cols, density_count):
    n = lax.axis_size("row")
    slots, blk, width = row_aux_tiles.shape
    window = 2 * REACH + 1
    span = width // CHUNKS
    vmem = pl.BlockSpec(memory_space=pltpu.VMEM)
    smem = pl.BlockSpec(memory_space=pltpu.SMEM)
    hbm = pl.BlockSpec(memory_space=pl.ANY)
    bf16 = jnp.bfloat16
    return pl.pallas_call(
        functools.partial(kernel, n),
        out_shape=jax.ShapeDtypeStruct((blk, window * blk), jnp.float32),
        in_specs=[hbm, hbm, smem, smem, vmem, smem, smem],
        out_specs=vmem,
        scratch_shapes=[
            pltpu.VMEM((slots, blk, width), bf16),
            pltpu.VMEM((slots, blk, width), bf16),
            pltpu.VMEM((width, width), bf16),
            pltpu.VMEM((slots, blk, width), bf16),
            pltpu.VMEM((slots, blk, width), bf16),
            pltpu.VMEM((slots, 256, 256), bf16),
            pltpu.VMEM((CHUNKS, blk, span), bf16),
            pltpu.VMEM((10, CHUNKS, blk, span), bf16),
            pltpu.VMEM((window, blk, blk), jnp.float32),
            pltpu.VMEM((10, blk // 2, 2 * blk), jnp.float32),
            pltpu.VMEM((window, blk // 2, 2 * blk), jnp.float32),
            pltpu.SemaphoreType.DMA((2,)),
            pltpu.SemaphoreType.DMA((6, CHUNKS)),
            pltpu.SemaphoreType.DMA((4, CHUNKS)),
            pltpu.SemaphoreType.DMA((10, CHUNKS)),
            pltpu.SemaphoreType.DMA((10,)),
            pltpu.SemaphoreType.DMA((window,)),
        ],
        compiler_params=pltpu.CompilerParams(
            collective_id=0, has_side_effects=True, vmem_limit_bytes=40 * 2**20),
        cost_estimate=pl.CostEstimate(flops=2 * 10**9, bytes_accessed=3 * 2**20, transcendentals=0),
    )(row_aux_tiles, partner_aux_tiles, tile_partner, tile_count, density_blocks, density_cols,
      density_count)


def solution(mesh):
    in_specs = (
        P(("groups", "row"), None, None),
        P(("groups", "row"), None, None),
        P(("groups", "row")),
        P(("groups", "row")),
        P(("groups", "row"), None, None),
        P(("groups", "row")),
        P(("groups", "row")),
    )
    out_specs = P(("groups", "row"), None)
    return jax.shard_map(body, mesh=mesh, in_specs=in_specs, out_specs=out_specs, check_vma=False)
```

time: 134 us -> 33.9 us (0.25)
  the two profiles are of different devices: /device:TPU:5 before, /device:TPU:0 now
where the time goes in v1:
time: 33.9 us; the launch traced here: 33.6 us
  Pallas kernels  28.2 us (83%)
  local copies, waits for them, and re-layouts  4.03 us (12%)
  between operations  1.37 us (4%)
    pallas_call x1, Pallas kernels, body(): pl.pallas_call(functools.partial(kernel, n), out_shape=jax.ShapeDtypeStru...  28.2 us
    unnamed x11, local copies, waits for them, and re-layouts  4.03 us

profile of v1, /device:TPU:0, one launch (start us, length us, event | category | flops | bytes accessed | tf_op | source)
XLA Modules:
  0.0 33.6 jit_solution(10121452057984299850)
XLA Ops:
  0.7 0.0 copy-start.3
  0.7 0.0 copy-start.4
  1.3 0.0 copy-done.3
  1.3 0.0 copy-done.4
  1.4 0.0 copy-start
  1.4 1.2 %copy-done = bf16[8,64,1024]{2,1,0:T(8,128)(2,1)S(1)} copy-done((bf16[8,64,1024]{2,1,0:T(8,128)(2,1)S(1)}, bf16[8,64,1024]{2,1,0:T(8,128)(2,1)}, u32[]{:S(2)}) %copy-start) | copy-done | bytes 1048600
  2.6 0.0 copy-start.1
  2.6 1.2 %copy-done.1 = bf16[8,64,1024]{2,1,0:T(8,128)(2,1)S(1)} copy-done((bf16[8,64,1024]{2,1,0:T(8,128)(2,1)S(1)}, bf16[8,64,1024]{2,1,0:T(8,128)(2,1)}, u32[]{:S(2)}) %copy-start.1) | copy-done | bytes 1048600
  3.8 0.0 copy-start.2
  3.8 0.9 %copy-done.2 = bf16[8,64,64]{2,1,0:T(8,128)(2,1)S(1)} copy-done((bf16[8,64,64]{2,1,0:T(8,128)(2,1)S(1)}, bf16[8,64,64]{2,1,0:T(8,128)(2,1)}, u32[]{:S(2)}) %copy-start.2) | copy-done | bytes 65560
  4.7 28.2 %shard_map.73 = f32[64,704]{1,0:T(8,128)S(1)} custom-call(bf16[8,64,1024]{2,1,0:T(8,128)(2,1)S(1)} %copy-done, bf16[8,64,1024]{2,1,0:T(8,128)(2,1)S(1)} %copy-done.1, s32[8]{0:T(128)S(1)} %copy-done.3, s32[1]{0:T(128)S(6)} %copy.9.count, bf16[8,64,64]{2,1,0:T(8,128)(2,1)S(1)} %copy-done.2, s32[8]{0:T(128)S(1)} %copy-done.4, s32[1]{0:T(128)S(6)} %copy.10.dense_count), custom_call_target="tpu_custom_call" | custom-call | flops 2000000000 | bytes 3145728 | tf_op jit(solution)/shard_map/pallas_call | solution.py:181
  33.0 0.7 %copy.11 = f32[64,704]{1,0:T(8,128)} copy(f32[64,704]{1,0:T(8,128)S(1)} %shard_map.73) | data formatting | bytes 360448
Async XLA Ops:
  0.7 0.7 %copy-start.3 = (s32[8]{0:T(128)S(1)}, s32[8]{0:T(128)}, u32[]{:S(2)}) copy-start(s32[8]{0:T(128)} %partner.1) | copy-start | bytes 100
  0.7 0.7 %copy-start.4 = (s32[8]{0:T(128)S(1)}, s32[8]{0:T(128)}, u32[]{:S(2)}) copy-start(s32[8]{0:T(128)} %cols.1) | copy-start | bytes 100
  1.4 1.2 %copy-start = (bf16[8,64,1024]{2,1,0:T(8,128)(2,1)S(1)}, bf16[8,64,1024]{2,1,0:T(8,128)(2,1)}, u32[]{:S(2)}) copy-start(bf16[8,64,1024]{2,1,0:T(8,128)(2,1)} %row_hbm.1) | copy-start | bytes 3145732
  2.6 1.2 %copy-start.1 = (bf16[8,64,1024]{2,1,0:T(8,128)(2,1)S(1)}, bf16[8,64,1024]{2,1,0:T(8,128)(2,1)}, u32[]{:S(2)}) copy-start(bf16[8,64,1024]{2,1,0:T(8,128)(2,1)} %pair_hbm.1) | copy-start | bytes 3145732
  3.8 0.9 %copy-start.2 = (bf16[8,64,64]{2,1,0:T(8,128)(2,1)S(1)}, bf16[8,64,64]{2,1,0:T(8,128)(2,1)}, u32[]{:S(2)}) copy-start(bf16[8,64,64]{2,1,0:T(8,128)(2,1)} %density.1) | copy-start | bytes 196612

commit v2 on v1

--- a/solution.py
+++ b/solution.py
@@ -8,13 +8,12 @@
 from jax.sharding import PartitionSpec as P
 
 REACH = 5
-CHUNKS = 2
-DIRECT = (2, -2, 4, -4)
+CHUNKS = 4
 N_T = (((1,), (1,)), ((), ()))
 
 
-def kernel(n, row_hbm, pair_hbm, partner, count, density, cols, dense_count, out,
-           row_v, pair_v, perm, row_p, pair_p, weights, mine, near, half, leaving, mirror,
+def kernel(n, row_hbm, pair_hbm, partner, count, density_hbm, cols, dense_count, out,
+           row_v, pair_v, density, perm, row_p, pair_p, weights, mine, near, half, leaving, mirror,
            load_sem, send_sem, pass_sem, near_sem, back_sem, mirror_sem):
     slots, blk, width = row_v.shape
     dense = density.shape[0]
@@ -26,13 +25,18 @@
 
     me = lax.axis_index("row")
     core = lax.rem(me, 2)
+    column = lax.rem(lax.div(me, 2), 2)
     side = 1 - 2 * core
+    ahead = 1 - 2 * column
+    inner = lax.rem(core + column, 2)
 
     def at(offset):
         return {"row": lax.rem(me + offset + n, n)}
 
     load_row = pltpu.make_async_copy(row_hbm, row_v, load_sem.at[0])
     load_pair = pltpu.make_async_copy(pair_hbm, pair_v, load_sem.at[1])
+    load_density = pltpu.make_async_copy(density_hbm, density, load_sem.at[2])
+    load_density.start()
     load_row.start()
     load_pair.start()
     barrier = pltpu.get_barrier_semaphore()
@@ -48,6 +52,7 @@
         perm[:, tile * 128:(tile + 1) * 128] = jnp.where(
             goes_to == lane + tile * 128, 1.0, 0.0).astype(jnp.bfloat16)
 
+    load_density.wait()
     live_tiles = count[0]
     live_dense = dense_count[0]
     zero = jnp.zeros((blk, blk), jnp.bfloat16)
@@ -78,6 +83,17 @@
             slots, blk, group)
 
     sends = []
+
+    def to_slot(source, slot, h, sem, offset):
+        return pltpu.make_async_remote_copy(
+            src_ref=source, dst_ref=near.at[slot, h], send_sem=sem, recv_sem=near_sem.at[slot, h],
+            device_id=at(offset), device_id_type=pl.DeviceIdType.MESH)
+
+    def put(source, slot, h, sem, offset):
+        copy = to_slot(source, slot, h, sem, offset)
+        copy.start()
+        sends.append(copy)
+
     load_row.wait()
     for h in range(CHUNKS):
         for step in range(per_chunk):
@@ -90,24 +106,35 @@
             mine[h, :, step * group:(step + 1) * group] = total.astype(jnp.bfloat16)
         if h == 0:
             pl.semaphore_wait(barrier, 2 * REACH)
-        for slot, offset in ((0, -2), (1, 2), (2, -4), (3, 4), (4, side), (9, -5 * side)):
-            number = slot if slot < 5 else 5
-            copy = pltpu.make_async_remote_copy(
-                src_ref=mine.at[h], dst_ref=near.at[slot, h],
-                send_sem=send_sem.at[number, h], recv_sem=near_sem.at[slot, h],
-                device_id=at(offset), device_id_type=pl.DeviceIdType.MESH)
-            copy.start()
-            sends.append(copy)
+        for number, slot, offset in ((0, 1, -4 * ahead), (1, 2, 4 * ahead), (2, 0, 2 * ahead),
+                                     (3, 4, side)):
+            put(mine.at[h], slot, h, send_sem.at[number, h], offset)
+        far = to_slot(mine.at[h], 9, h, send_sem.at[4, h], -5 * ahead)
+
+        @pl.when(inner == 0)
+        def _():
+            far.start()
+
+        sends.append(far)
 
     def arrived(slot, h):
-        pltpu.make_async_remote_copy(
-            src_ref=mine.at[h], dst_ref=near.at[slot, h],
-            send_sem=send_sem.at[0, h], recv_sem=near_sem.at[slot, h],
-            device_id=at(side), device_id_type=pl.DeviceIdType.MESH).wait_recv()
+        to_slot(mine.at[h], slot, h, send_sem.at[0, h], side).wait_recv()
+
+    def pass_on(h):
+        for slot in (1, 2, 0, 3):
+            arrived(slot, h)
+            if slot == 1:
+                put(near.at[1, h], 3, h, pass_sem.at[4, h], 2 * ahead)
+            if slot == 2:
+                @pl.when(inner == 1)
+                def _():
+                    to_slot(near.at[2, h], 9, h, send_sem.at[4, h], ahead).start()
+            put(near.at[slot, h], 5 + slot, h, pass_sem.at[slot, h], side)
 
     load_pair.wait()
     for g in range(n_group):
         reorder(pair_v, pair_p, g)
+        pass_on(g)
 
     where = [lax.rem(partner[t] - me + REACH + n, n) - REACH for t in range(slots)]
 
@@ -127,18 +154,9 @@
     own = term(0, lambda h: mine[h])
     half[REACH] = own + own.T
 
-    for h in range(CHUNKS):
-        for slot in range(4):
-            arrived(slot, h)
-            copy = pltpu.make_async_remote_copy(
-                src_ref=near.at[slot, h], dst_ref=near.at[5 + slot, h],
-                send_sem=pass_sem.at[slot, h], recv_sem=near_sem.at[5 + slot, h],
-                device_id=at(side), device_id_type=pl.DeviceIdType.MESH)
-            copy.start()
-            sends.append(copy)
-
-    order = [(4, side), (0, 2), (1, -2), (5, 2 + side), (6, -2 + side), (2, 4), (3, -4),
-             (7, 4 + side), (8, -4 + side), (9, -5 * side)]
+    order = [(4, side), (0, 2 * ahead), (1, 4 * ahead), (2, -4 * ahead), (3, -2 * ahead),
+             (5, side + 2 * ahead), (6, side + 4 * ahead), (7, side - 4 * ahead),
+             (8, side - 2 * ahead), (9, -5 * side)]
     for slot, offset in order:
         if slot >= 4:
             for h in range(CHUNKS):
@@ -172,6 +190,7 @@
          density_cols, density_count):
     n = lax.axis_size("row")
     slots, blk, width = row_aux_tiles.shape
+    dense = density_blocks.shape[0]
     window = 2 * REACH + 1
     span = width // CHUNKS
     vmem = pl.BlockSpec(memory_space=pltpu.VMEM)
@@ -181,11 +200,12 @@
     return pl.pallas_call(
         functools.partial(kernel, n),
         out_shape=jax.ShapeDtypeStruct((blk, window * blk), jnp.float32),
-        in_specs=[hbm, hbm, smem, smem, vmem, smem, smem],
+        in_specs=[hbm, hbm, smem, smem, hbm, smem, smem],
         out_specs=vmem,
         scratch_shapes=[
             pltpu.VMEM((slots, blk, width), bf16),
             pltpu.VMEM((slots, blk, width), bf16),
+            pltpu.VMEM((dense, blk, blk), bf16),
             pltpu.VMEM((width, width), bf16),
             pltpu.VMEM((slots, blk, width), bf16),
             pltpu.VMEM((slots, blk, width), bf16),
@@ -195,15 +215,15 @@
             pltpu.VMEM((window, blk, blk), jnp.float32),
             pltpu.VMEM((10, blk // 2, 2 * blk), jnp.float32),
             pltpu.VMEM((window, blk // 2, 2 * blk), jnp.float32),
-            pltpu.SemaphoreType.DMA((2,)),
-            pltpu.SemaphoreType.DMA((6, CHUNKS)),
-            pltpu.SemaphoreType.DMA((4, CHUNKS)),
+            pltpu.SemaphoreType.DMA((3,)),
+            pltpu.SemaphoreType.DMA((5, CHUNKS)),
+            pltpu.SemaphoreType.DMA((5, CHUNKS)),
             pltpu.SemaphoreType.DMA((10, CHUNKS)),
             pltpu.SemaphoreType.DMA((10,)),
             pltpu.SemaphoreType.DMA((window,)),
         ],
         compiler_params=pltpu.CompilerParams(
-            collective_id=0, has_side_effects=True, vmem_limit_bytes=40 * 2**20),
+            collective_id=0, has_side_effects=True, vmem_limit_bytes=60 * 2**20),
         cost_estimate=pl.CostEstimate(flops=2 * 10**9, bytes_accessed=3 * 2**20, transcendentals=0),
     )(row_aux_tiles, partner_aux_tiles, tile_partner, tile_count, density_blocks, density_cols,
       density_count)

time: 33.9 us -> 37.4 us (1.10)
  the two profiles are of different devices: /device:TPU:0 before, /device:TPU:1 now
where the time goes in v2:
time: 37.4 us; the launch traced here: 37.3 us
  Pallas kernels  34.3 us (92%)
  local copies, waits for them, and re-layouts  1.62 us (4%)
  between operations  1.3 us (3%)
    pallas_call x1, Pallas kernels, body(): pl.pallas_call(functools.partial(kernel, n), out_shape=jax.ShapeDtypeStru...  34.3 us
    unnamed x1, local copies, waits for them, and re-layouts  1.62 us

profile of v2, /device:TPU:1, one launch (start us, length us, event | category | flops | bytes accessed | tf_op | source)
XLA Modules:
  0.0 37.3 jit_solution(14757081460587681682)
XLA Ops:
  1.3 34.3 %shard_map.73 = f32[64,704]{1,0:T(8,128)} custom-call(bf16[8,64,1024]{2,1,0:T(8,128)(2,1)} %row_hbm.1, bf16[8,64,1024]{2,1,0:T(8,128)(2,1)} %pair_hbm.1, s32[8]{0:T(128)} %partner.1, s32[1]{0:T(128)S(6)} %copy.9.count, bf16[8,64,64]{2,1,0:T(8,128)(2,1)} %density_hbm.1, s32[8]{0:T(128)} %cols.1, s32[1]{0:T(128)S(6)} %copy.10.dense_count), custom_call_target="tpu_custom_call" | custom-call | flops 2000000000 | bytes 3145728 | tf_op jit(solution)/shard_map/pallas_call | solution.py:200
  35.6 1.6 %copy.11 = f32[64,704]{1,0:T(8,128)} copy(f32[64,704]{1,0:T(8,128)} %shard_map.73) | data formatting | bytes 360448

commit v3 on v2

--- a/solution.py
+++ b/solution.py
@@ -8,7 +8,7 @@
 from jax.sharding import PartitionSpec as P
 
 REACH = 5
-CHUNKS = 4
+CHUNKS = 2
 N_T = (((1,), (1,)), ((), ()))
 
 
@@ -120,8 +120,10 @@
     def arrived(slot, h):
         to_slot(mine.at[h], slot, h, send_sem.at[0, h], side).wait_recv()
 
-    def pass_on(h):
-        for slot in (1, 2, 0, 3):
+    def pass_on(step):
+        for slot, h in ((1, step), (2, step), (0, step), (3, step - 1)):
+            if h < 0 or h >= CHUNKS:
+                continue
             arrived(slot, h)
             if slot == 1:
                 put(near.at[1, h], 3, h, pass_sem.at[4, h], 2 * ahead)
@@ -134,7 +136,8 @@
     load_pair.wait()
     for g in range(n_group):
         reorder(pair_v, pair_p, g)
-        pass_on(g)
+        if (g + 1) % per_chunk == 0:
+            pass_on(g // per_chunk)
 
     where = [lax.rem(partner[t] - me + REACH + n, n) - REACH for t in range(slots)]
 
@@ -154,10 +157,10 @@
     own = term(0, lambda h: mine[h])
     half[REACH] = own + own.T
 
-    order = [(4, side), (0, 2 * ahead), (1, 4 * ahead), (2, -4 * ahead), (3, -2 * ahead),
-             (5, side + 2 * ahead), (6, side + 4 * ahead), (7, side - 4 * ahead),
+    order = [(4, side), (0, 2 * ahead), (1, 4 * ahead), (2, -4 * ahead), (5, side + 2 * ahead),
+             (3, -2 * ahead), (6, side + 4 * ahead), (7, side - 4 * ahead),
              (8, side - 2 * ahead), (9, -5 * side)]
-    for slot, offset in order:
+    def settle(slot, offset):
         if slot >= 4:
             for h in range(CHUNKS):
                 arrived(slot, h)
@@ -171,6 +174,12 @@
             device_id=at(offset), device_id_type=pl.DeviceIdType.MESH)
         copy.start()
         sends.append(copy)
+
+    for slot, offset in order[:2]:
+        settle(slot, offset)
+    pass_on(CHUNKS)
+    for slot, offset in order[2:]:
+        settle(slot, offset)
 
     for s in range(2 * REACH + 1):
         value = half[s]

time: 37.4 us -> 29.6 us (0.79)
  Pallas kernels: 34.3 us -> 26.5 us
    pallas_call x1, Pallas kernels: 34.3 us -> 26.5 us  [body(): pl.pallas_call(functools.partial(kernel, n), out_shape=jax.ShapeDtypeStru...]
where the time goes in v3:
time: 29.6 us; the launch traced here: 29.4 us
  Pallas kernels  26.5 us (90%)
  local copies, waits for them, and re-layouts  1.62 us (5%)
  between operations  1.3 us (4%)
    pallas_call x1, Pallas kernels, body(): pl.pallas_call(functools.partial(kernel, n), out_shape=jax.ShapeDtypeStru...  26.5 us
    unnamed x1, local copies, waits for them, and re-layouts  1.62 us

profile of v3, /device:TPU:1, one launch (start us, length us, event | category | flops | bytes accessed | tf_op | source)
XLA Modules:
  0.0 29.4 jit_solution(12747466069094549981)
XLA Ops:
  1.3 26.5 %shard_map.73 = f32[64,704]{1,0:T(8,128)} custom-call(bf16[8,64,1024]{2,1,0:T(8,128)(2,1)} %row_hbm.1, bf16[8,64,1024]{2,1,0:T(8,128)(2,1)} %pair_hbm.1, s32[8]{0:T(128)} %partner.1, s32[1]{0:T(128)S(6)} %copy.9.count, bf16[8,64,64]{2,1,0:T(8,128)(2,1)} %density_hbm.1, s32[8]{0:T(128)} %cols.1, s32[1]{0:T(128)S(6)} %copy.10.dense_count), custom_call_target="tpu_custom_call" | custom-call | flops 2000000000 | bytes 3145728 | tf_op jit(solution)/shard_map/pallas_call | solution.py:209
  27.8 1.6 %copy.11 = f32[64,704]{1,0:T(8,128)} copy(f32[64,704]{1,0:T(8,128)} %shard_map.73) | data formatting | bytes 360448

commit v4 on v3

--- a/solution.py
+++ b/solution.py
@@ -13,7 +13,7 @@
 
 
 def kernel(n, row_hbm, pair_hbm, partner, count, density_hbm, cols, dense_count, out,
-           row_v, pair_v, density, perm, row_p, pair_p, weights, mine, near, half, leaving, mirror,
+           row_v, pair_v, density, perm, row_p, pair_p, weights, mine, near, first, half, leaving, mirror,
            load_sem, send_sem, pass_sem, near_sem, back_sem, mirror_sem):
     slots, blk, width = row_v.shape
     dense = density.shape[0]
@@ -141,30 +141,44 @@
 
     where = [lax.rem(partner[t] - me + REACH + n, n) - REACH for t in range(slots)]
 
-    def term(offset, block):
+    def chosen(offset):
         index = jnp.int32(0)
         found = jnp.int32(0)
         for t in range(slots):
             hit = ((where[t] == offset) & (t < live_tiles)).astype(jnp.int32)
             index += hit * t
             found += hit
-        total = jnp.zeros((blk, blk), jnp.float32)
-        for h in range(CHUNKS):
-            total += lax.dot_general(pair_p[index, :, h * span:(h + 1) * span], block(h), N_T,
-                                     preferred_element_type=jnp.float32)
-        return total * found.astype(jnp.float32)
-
-    own = term(0, lambda h: mine[h])
+        return index, found.astype(jnp.float32)
+
+    def term(index, h, block):
+        return lax.dot_general(pair_p[index, :, h * span:(h + 1) * span], block, N_T,
+                               preferred_element_type=jnp.float32)
+
+    index, found = chosen(0)
+    own = sum(term(index, h, mine[h]) for h in range(CHUNKS)) * found
     half[REACH] = own + own.T
 
     order = [(4, side), (0, 2 * ahead), (1, 4 * ahead), (2, -4 * ahead), (5, side + 2 * ahead),
              (3, -2 * ahead), (6, side + 4 * ahead), (7, side - 4 * ahead),
              (8, side - 2 * ahead), (9, -5 * side)]
+    picks = {slot: chosen(offset) for slot, offset in order}
+    started = []
+
+    def begin(slot):
+        if slot >= 4:
+            for h in range(CHUNKS - 1):
+                arrived(slot, h)
+        index, _ = picks[slot]
+        first[slot] = sum(term(index, h, near[slot, h]) for h in range(CHUNKS - 1))
+        started.append(slot)
+
     def settle(slot, offset):
+        if slot not in started:
+            begin(slot)
         if slot >= 4:
-            for h in range(CHUNKS):
-                arrived(slot, h)
-        value = term(offset, lambda h: near[slot, h])
+            arrived(slot, CHUNKS - 1)
+        index, found = picks[slot]
+        value = (first[slot] + term(index, CHUNKS - 1, near[slot, CHUNKS - 1])) * found
         half[REACH + offset] = value
         turned = value.T
         leaving[slot] = jnp.concatenate([turned[:blk // 2], turned[blk // 2:]], axis=1)
@@ -177,11 +191,13 @@
 
     for slot, offset in order[:2]:
         settle(slot, offset)
+    for slot in (1, 2, 3, 6, 7, 9):
+        begin(slot)
     pass_on(CHUNKS)
     for slot, offset in order[2:]:
         settle(slot, offset)
 
-    for s in range(2 * REACH + 1):
+    for s in sorted(range(2 * REACH + 1), key=lambda s: abs(s - REACH)):
         value = half[s]
         if s != REACH:
             pltpu.make_async_remote_copy(
@@ -221,6 +237,7 @@
             pltpu.VMEM((slots, 256, 256), bf16),
             pltpu.VMEM((CHUNKS, blk, span), bf16),
             pltpu.VMEM((10, CHUNKS, blk, span), bf16),
+            pltpu.VMEM((10, blk, blk), jnp.float32),
             pltpu.VMEM((window, blk, blk), jnp.float32),
             pltpu.VMEM((10, blk // 2, 2 * blk), jnp.float32),
             pltpu.VMEM((window, blk // 2, 2 * blk), jnp.float32),

time: 29.6 us -> 29.4 us (level)
  Pallas kernels: 26.5 us -> 26.2 us
where the time goes in v4:
time: 29.4 us; the launch traced here: 29.2 us
  Pallas kernels  26.2 us (89%)
  local copies, waits for them, and re-layouts  1.62 us (6%)
  between operations  1.3 us (4%)
    pallas_call x1, Pallas kernels, body(): pl.pallas_call(functools.partial(kernel, n), out_shape=jax.ShapeDtypeStru...  26.2 us
    unnamed x1, local copies, waits for them, and re-layouts  1.62 us

profile of v4, /device:TPU:1, one launch (start us, length us, event | category | flops | bytes accessed | tf_op | source)
XLA Modules:
  0.0 29.2 jit_solution(15917498340356281106)
XLA Ops:
  1.3 26.2 %shard_map.73 = f32[64,704]{1,0:T(8,128)} custom-call(bf16[8,64,1024]{2,1,0:T(8,128)(2,1)} %row_hbm.1, bf16[8,64,1024]{2,1,0:T(8,128)(2,1)} %pair_hbm.1, s32[8]{0:T(128)} %partner.1, s32[1]{0:T(128)S(6)} %copy.9.count, bf16[8,64,64]{2,1,0:T(8,128)(2,1)} %density_hbm.1, s32[8]{0:T(128)} %cols.1, s32[1]{0:T(128)S(6)} %copy.10.dense_count), custom_call_target="tpu_custom_call" | custom-call | flops 2000000000 | bytes 3145728 | tf_op jit(solution)/shard_map/pallas_call | solution.py:225
  27.6 1.6 %copy.11 = f32[64,704]{1,0:T(8,128)} copy(f32[64,704]{1,0:T(8,128)} %shard_map.73) | data formatting | bytes 360448
